TPU v7x, 32 devices: a whole 2x2x4 slice. The times are simulated.
32 devices in a mesh: fsdp: 8 (over y, x, core), tensor: 4 (over z).
Axes of the slice: x: 2, y: 2, z: 4, core: 2. Of those that a mesh axis runs over, the one named last changes fastest.
Arguments:
- hidden_t: bfloat16 [28672, 512], P('fsdp', 'tensor'), may hold values from -6 to 6
- down_weight: bfloat16 [28672, 4096], P('fsdp', 'tensor'), may hold values from -0.03125 to 0.03125
- probe: bfloat16 [28672, 4096], P('fsdp', 'tensor'), may hold values from -5 to 5
- grad_moment: bfloat16 [28672, 4096], P('fsdp', 'tensor'), may hold values from -0.0059814453 to 0.0059814453
- curv_moment: bfloat16 [28672, 4096], P('fsdp', 'tensor'), may hold values from 0.0099487305 to 0.099609375
- target: bfloat16 [512, 4096], P('fsdp', 'tensor'), may hold values from -6 to 6
Outputs:
- new_grad_moment: bfloat16 [28672, 4096], P('fsdp', 'tensor')
- new_curv_moment: bfloat16 [28672, 4096], P('fsdp', 'tensor')
- update: bfloat16 [28672, 4096], P('fsdp', 'tensor')
All inputs are finite; a program needn't handle non-finite values.
Results may differ from a plain program's by a relative error of at most 0.0056.
Values may be sent and summed in bfloat16 or wider, within the bound.
A program may use at most 192 MiB of HBM per device.

v0:
```python
import jax
import jax.numpy as jnp
from jax import lax
from jax.sharding import PartitionSpec as P

BETA_ONE = 0.965
BETA_TWO = 0.99
RHO_SCALE = 0.02
EPS_FLOOR = 0.0005


def cotangents(summed, target_rows, col_width, token_count):
    adjoint = ((summed[:, :col_width] - target_rows.astype(jnp.float32)) / token_count).astype(
        jnp.bfloat16
    )
    tangent_adjoint = (summed[:, col_width:] / token_count).astype(jnp.bfloat16)
    return jnp.concatenate([adjoint, tangent_adjoint], axis=1)


def shards(hidden_t, down_weight, probe, grad_moment, curv_moment, target):
    gathered = lax.all_gather(hidden_t, "tensor", axis=1, tiled=True)
    col_width = down_weight.shape[1]
    token_count = gathered.shape[1]
    paired = jnp.concatenate([down_weight, probe], axis=1)
    partial_out = lax.dot_general(
        gathered, paired, (((0,), (0,)), ((), ())), preferred_element_type=jnp.float32
    )
    totals = lax.psum(partial_out, "fsdp")
    target_all = lax.all_gather(target, "fsdp", axis=0, tiled=True)
    stacked = cotangents(totals, target_all, col_width, token_count)
    products = jnp.dot(gathered, stacked, preferred_element_type=jnp.float32)
    gradient = products[:, :col_width]
    hess_probe = products[:, col_width:]
    estimate = probe.astype(jnp.float32) * hess_probe
    moment_next = BETA_ONE * grad_moment.astype(jnp.float32) + (1.0 - BETA_ONE) * gradient
    curv_next = BETA_TWO * curv_moment.astype(jnp.float32) + (1.0 - BETA_TWO) * estimate
    raw_ratio = moment_next / jnp.maximum(RHO_SCALE * curv_next, EPS_FLOOR)
    update = jnp.clip(raw_ratio, -1.0, 1.0)
    return (
        moment_next.astype(jnp.bfloat16),
        curv_next.astype(jnp.bfloat16),
        update.astype(jnp.bfloat16),
    )


def solution(mesh):
    in_specs = (
        P("fsdp", "tensor"),
        P("fsdp", "tensor"),
        P("fsdp", "tensor"),
        P("fsdp", "tensor"),
        P("fsdp", "tensor"),
        P("fsdp", "tensor"),
    )
    out_specs = (P("fsdp", "tensor"), P("fsdp", "tensor"), P("fsdp", "tensor"))
    return jax.shard_map(shards, mesh=mesh, in_specs=in_specs, out_specs=out_specs, check_vma=False)
```

profile of v0, /device:TPU:0, one launch (start us, length us, event | category | flops | bytes accessed | tf_op | source)
XLA Modules:
  0.0 273.3 jit_solution(6230435863053550682)
XLA Ops:
  7.2 0.0 all-gather.3.cloned.1.call-start
  7.2 0.7 all-gather.3.cloned.1.call-update
  7.9 0.0 all-gather.5.cloned.1.call-start
  7.9 0.7 all-gather.5.cloned.1.call-update
  8.6 0.0 all-reduce.2.cloned.1.call-start
  8.7 75.6 %all-gather.3.cloned.1.call-done = bf16[3584,512]{1,0:T(8,128)(2,1)} async-done(((bf16[3584,128]{1,0:T(8,128)(2,1)}), bf16[3584,512]{1,0:T(8,128)(2,1)}) %all-gather.3.cloned.1.call-update) | async-done | bytes 3670032 | tf_op jit(solution)/shard_map/all_gather | solution.py:21
  84.3 16.0 %fusion.8 = f32[512,2048]{0,1:T(8,128)} fusion(bf16[3584,512]{1,0:T(8,128)(2,1)} %all-gather.3.cloned.1.call-done, bf16[3584,1024]{1,0:T(8,128)(2,1)} %param.8, bf16[3584,1024]{1,0:T(8,128)(2,1)} %param.7), kind=kOutput, calls=%fused_computation.12 | convolution fusion | flops 7545552896 | bytes 22544384 | tf_op jit(solution)/shard_map/dot_general | solution.py:25
  100.3 0.0 all-reduce.2.cloned.1.call-update
  100.3 10.2 %copy.19 = bf16[3584,1024]{0,1:T(8,128)(2,1)} copy(bf16[3584,1024]{1,0:T(8,128)(2,1)} %param.8) | data formatting | bytes 14680064 | tf_op args[2]
  110.6 10.2 %copy.16 = bf16[3584,1024]{0,1:T(8,128)(2,1)} copy(bf16[3584,1024]{1,0:T(8,128)(2,1)} %param.9) | data formatting | bytes 14680064 | tf_op args[3]
  120.7 10.0 %copy.18 = bf16[3584,1024]{0,1:T(8,128)(2,1)} copy(bf16[3584,1024]{1,0:T(8,128)(2,1)} %param.10) | data formatting | bytes 14680064 | tf_op args[4]
  130.8 0.0 all-gather.5.cloned.1.call-done
  130.8 1.5 copy.17
  132.3 59.9 %all-reduce.2.cloned.1.call-done = f32[512,2048]{0,1:T(8,128)} async-done(((f32[512,2048]{0,1:T(8,128)}), f32[512,2048]{0,1:T(8,128)}) %all-reduce.2.cloned.1.call-update) | async-done | bytes 4194320 | tf_op jit(solution)/shard_map/psum | solution.py:28
  192.2 0.0 slice-start
  192.2 3.0 %fusion.14 = (bf16[512,1024]{0,1:T(8,128)(2,1)S(1)}, bf16[512,1024]{0,1:T(8,128)(2,1)S(1)}) fusion(f32[512,2048]{0,1:T(8,128)} %all-reduce.2.cloned.1.call-done, bf16[512,1024]{0,1:T(8,128)(2,1)S(1)} %copy.17), kind=kLoop, calls=%fused_computation.18 | loop fusion | flops 3145728 | bytes 7340032 | tf_op jit(solution)/shard_map/convert_element_type | solution.py:13
  195.2 0.0 slice-start.1
  195.3 16.8 %convolution_bitcast_fusion = f32[3584,2048]{0,1:T(8,128)} fusion(bf16[3584,512]{1,0:T(8,128)(2,1)} %all-gather.3.cloned.1.call-done, bf16[512,1024]{0,1:T(8,128)(2,1)S(1)} %get-tuple-element.13, bf16[512,1024]{0,1:T(8,128)(2,1)S(1)} %get-tuple-element.12), kind=kOutput, calls=%fused_computation | convolution fusion | flops 7520387072 | bytes 35127296 | tf_op jit(solution)/shard_map/dot_general | solution.py:31
  212.1 0.0 slice-done
  212.1 0.0 slice-done.1
  212.1 23.6 %clamp_convert_fusion = (bf16[3584,1024]{0,1:T(8,128)(2,1)}, bf16[3584,1024]{0,1:T(8,128)(2,1)}, bf16[3584,1024]{0,1:T(8,128)(2,1)}) fusion(f32[3584,2048]{0,1:T(8,128)} %convolution_bitcast_fusion, bf16[3584,1024]{0,1:T(8,128)(2,1)} %copy.16, bf16[3584,1024]{0,1:T(8,128)(2,1)S(1)} %bitcast.7, bf16[3584,1024]{0,1:T(8,128)(2,1)} %copy.18), kind=kLoop, calls=%fused_computation.10 | loop fusion | flops 62390272 | bytes 73400320 | tf_op jit(solution)/shard_map/convert_element_type | solution.py:42
  235.6 10.4 %copy.20 = bf16[3584,1024]{1,0:T(8,128)(2,1)} copy(bf16[3584,1024]{0,1:T(8,128)(2,1)} %get-tuple-element.11) | data formatting | bytes 14680064
  246.0 10.4 %copy.21 = bf16[3584,1024]{1,0:T(8,128)(2,1)} copy(bf16[3584,1024]{0,1:T(8,128)(2,1)} %get-tuple-element.10) | data formatting | bytes 14680064
  256.4 10.4 %copy.22 = bf16[3584,1024]{1,0:T(8,128)(2,1)} copy(bf16[3584,1024]{0,1:T(8,128)(2,1)} %get-tuple-element.9) | data formatting | bytes 14680064
  (1 shorter events, 0.0 us)
Async XLA Ops:
  7.2 77.1 %all-gather.3.cloned.1.call-start = ((), (), s32[]{:S(2)}) async-start(), calls=%async_computation | async-start | bytes 4587520 | tf_op jit(solution)/shard_map/all_gather | solution.py:21
  7.9 122.9 %all-gather.5.cloned.1.call-start = ((), (), s32[]{:S(2)}) async-start(), calls=%async_computation.2 | async-start | bytes 1179648 | tf_op jit(solution)/shard_map/all_gather | solution.py:29
  8.6 183.6 %all-reduce.2.cloned.1.call-start = ((), (), s32[]{:S(2)}) async-start(), calls=%async_computation.1 | async-start | bytes 8388608 | tf_op jit(solution)/shard_map/psum | solution.py:28
  192.2 19.9 %slice-start = ((s8[7340032]{0:T(1024)(128)(4,1)}), s8[4194304]{0:T(1024)(128)(4,1)S(1)}, s32[]{:S(2)}) async-start(s8[7340032]{0:T(1024)(128)(4,1)} %bitcast.6), calls=%async_computation.3 | async-start | bytes 8388608
  195.2 16.8 %slice-start.1 = ((s8[7340032]{0:T(1024)(128)(4,1)}), s8[3145728]{0:T(1024)(128)(4,1)S(1)}, s32[]{:S(2)}) async-start(s8[7340032]{0:T(1024)(128)(4,1)} %bitcast.6), calls=%async_computation.4 | async-start | bytes 6291456
Sparse Core Ops, SparseCore 0:
  9.6 74.6 all-gather.2
  86.2 21.6 all-gather.4
  111.2 80.9 all-reduce.1
where the time goes:
time: 275 us; the launch traced here: 273 us
  waiting for transfers between devices  137 us (50%)
  local copies, waits for them, and re-layouts  63.2 us (23%)
  matrix products  32.8 us (12%)
  other arithmetic  26.6 us (10%)
  between operations  13.8 us (5%)
    all_gather x1, waiting for transfers between devices, shards(): gathered = lax.all_gather(hidden_t, 'tensor', axis=1, tiled=True)  75.6 us
    unnamed x10, local copies, waits for them, and re-layouts  61.7 us
    psum x1, waiting for transfers between devices, shards(): totals = lax.psum(partial_out, 'fsdp')  59.9 us
    convert_element_type x1, other arithmetic, shards(): update.astype(jnp.bfloat16)  23.6 us
    dot_general x1, matrix products, shards(): products = jnp.dot(gathered, stacked, preferred_element_type=jnp.float32)  16.8 us
    dot_general x1, matrix products, shards(): lax.dot_general(gathered, paired, (((0,), (0,)), ((), ())), preferred_ele...  16 us
  transfers between devices with their start and end apart: 3, of which 2 were waited for; matrix products, arithmetic and copies ran while one was open for 18% of the time, Pallas kernels for 0%

commit v1 on v0

--- a/solution.py
+++ b/solution.py
@@ -9,6 +9,19 @@
 EPS_FLOOR = 0.0005
 
 
+def collect(x, axis, dim):
+    ways = lax.axis_size(axis)
+    up = [(d, (d + 1) % ways) for d in range(ways)]
+    down = [(d, (d - 1) % ways) for d in range(ways)]
+    earlier, later = ([x], [x])
+    for _ in range(ways // 2):
+        earlier.append(lax.ppermute(earlier[-1], axis, up))
+    for _ in range((ways - 1) // 2):
+        later.append(lax.ppermute(later[-1], axis, down))
+    line = jnp.concatenate([*earlier[::-1], *later[1:]], axis=dim)
+    return jnp.roll(line, (lax.axis_index(axis) - ways // 2) * x.shape[dim], axis=dim)
+
+
 def cotangents(summed, target_rows, col_width, token_count):
     adjoint = ((summed[:, :col_width] - target_rows.astype(jnp.float32)) / token_count).astype(
         jnp.bfloat16
@@ -18,7 +31,7 @@
 
 
 def shards(hidden_t, down_weight, probe, grad_moment, curv_moment, target):
-    gathered = lax.all_gather(hidden_t, "tensor", axis=1, tiled=True)
+    gathered = collect(hidden_t, "tensor", 1)
     col_width = down_weight.shape[1]
     token_count = gathered.shape[1]
     paired = jnp.concatenate([down_weight, probe], axis=1)

time: 275 us -> 227 us (0.83)
  local copies, waits for them, and re-layouts: 63.2 us -> 16.1 us
  starting transfers between devices: 0.11 us -> 6.98 us
  matrix products: 32.8 us -> 29 us
    all_gather x1 -> x0, waiting for transfers between devices: 75.6 us -> none  [shards(): gathered = lax.all_gather(hidden_t, 'tensor', axis=1, tiled=True)]
    ppermute x0 -> x3, waiting for transfers between devices: none -> 53.8 us  [the longest x2 44.2 us: collect(): earlier.append(lax.ppermute(earlier[-1], axis, up))]
    unnamed x10 -> x21, local copies, waits for them, and re-layouts: 61.7 us -> 14 us
    psum x1, waiting for transfers between devices: 59.9 us -> 81 us  [shards(): totals = lax.psum(partial_out, 'fsdp')]
    ppermute x0 -> x3, starting transfers between devices: none -> 6.9 us  [the longest x1 3.82 us: collect(): later.append(lax.ppermute(later[-1], axis, down))]
  transfers between devices with their start and end apart: 3 -> 5, of which waited for: 2 -> 4; matrix products, arithmetic and copies ran while one was open for 18% -> 13% of each run, Pallas kernels for 0% -> 0%
where the time goes in v1:
time: 227 us; the launch traced here: 226 us
  waiting for transfers between devices  135 us (59%)
  matrix products  29 us (13%)
  other arithmetic  25.2 us (11%)
  local copies, waits for them, and re-layouts  16.1 us (7%)
  between operations  14.1 us (6%)
  starting transfers between devices  6.98 us (3%)
    psum x1, waiting for transfers between devices, shards(): totals = lax.psum(partial_out, 'fsdp')  81 us
    ppermute x2, waiting for transfers between devices, collect(): earlier.append(lax.ppermute(earlier[-1], axis, up))  44.2 us
    convert_element_type x1, other arithmetic, shards(): update.astype(jnp.bfloat16)  20.9 us
    dot_general x1, matrix products, shards(): products = jnp.dot(gathered, stacked, preferred_element_type=jnp.float32)  15.5 us
    unnamed x21, local copies, waits for them, and re-layouts  14 us
    dot_general x1, matrix products, shards(): lax.dot_general(gathered, paired, (((0,), (0,)), ((), ())), preferred_ele...  13.5 us
    ppermute x1, waiting for transfers between devices, collect(): later.append(lax.ppermute(later[-1], axis, down))  9.63 us
  transfers between devices with their start and end apart: 5, of which 4 were waited for; matrix products, arithmetic and copies ran while one was open for 13% of the time, Pallas kernels for 0%

profile of v1, /device:TPU:0, one launch (start us, length us, event | category | flops | bytes accessed | tf_op | source)
XLA Modules:
  0.0 226.2 jit_solution(12162489615949591926)
XLA Ops:
  7.2 0.0 all-gather.2.cloned.1.call-start
  7.2 3.1 %collective-permute-start = (bf16[3584,128]{1,0:T(8,128)(2,1)}, bf16[3584,128]{1,0:T(8,128)(2,1)}, u32[]{:S(2)}, u32[]{:S(2)}) collective-permute-start(bf16[3584,128]{1,0:T(8,128)(2,1)} %param.6), channel_id=1, source_target_pairs={{0,1},{1,2},{2,3},{3,0},{4,5},{5,6},{6,7},{7,4},{8,9},{9,10},{10,1... | collective-permute-start | bytes 2752520 | tf_op jit(solution)/shard_map/ppermute | solution.py:18
  10.3 22.7 %collective-permute-done = bf16[3584,128]{1,0:T(8,128)(2,1)} collective-permute-done((bf16[3584,128]{1,0:T(8,128)(2,1)}, bf16[3584,128]{1,0:T(8,128)(2,1)}, u32[]{:S(2)}, u32[]{:S(2)}) %collective-permute-start) | collective-permute-done | bytes 917536 | tf_op jit(solution)/shard_map/ppermute | solution.py:18
  33.0 0.0 collective-permute-start.1
  33.0 3.8 %collective-permute-start.2 = (bf16[3584,128]{1,0:T(8,128)(2,1)}, bf16[3584,128]{1,0:T(8,128)(2,1)}, u32[]{:S(2)}, u32[]{:S(2)}) collective-permute-start(bf16[3584,128]{1,0:T(8,128)(2,1)} %param.6), channel_id=1, source_target_pairs={{0,3},{1,0},{2,1},{3,2},{4,7},{5,4},{6,5},{7,6},{8,11},{9,8},{10,9... | collective-permute-start | bytes 2752520 | tf_op jit(solution)/shard_map/ppermute | solution.py:20
  36.8 0.0 all-gather.2.cloned.1.call-update
  36.8 0.0 all-reduce.2.cloned.1.call-start
  36.9 0.0 slice-start
  36.9 0.0 copy-start
  36.9 21.5 %collective-permute-done.1 = bf16[3584,128]{1,0:T(8,128)(2,1)} collective-permute-done((bf16[3584,128]{1,0:T(8,128)(2,1)}, bf16[3584,128]{1,0:T(8,128)(2,1)}, u32[]{:S(2)}, u32[]{:S(2)}) %collective-permute-start.1) | collective-permute-done | bytes 917536 | tf_op jit(solution)/shard_map/ppermute | solution.py:18
  58.4 2.2 constant_dynamic-update-slice_fusion.7
  60.5 2.2 constant_dynamic-update-slice_fusion.6
  62.7 2.2 constant_dynamic-update-slice_fusion.5
  64.9 0.0 slice-start.1
  64.9 9.6 %collective-permute-done.2 = bf16[3584,128]{1,0:T(8,128)(2,1)} collective-permute-done((bf16[3584,128]{1,0:T(8,128)(2,1)}, bf16[3584,128]{1,0:T(8,128)(2,1)}, u32[]{:S(2)}, u32[]{:S(2)}) %collective-permute-start.2) | collective-permute-done | bytes 917536 | tf_op jit(solution)/shard_map/ppermute | solution.py:20
  74.5 2.2 constant_dynamic-update-slice_fusion.4
  76.7 2.2 constant_dynamic-update-slice_fusion.3
  78.8 2.2 constant_dynamic-update-slice_fusion.2
  81.0 0.0 copy-done
  81.0 1.0 constant_dynamic-update-slice_fusion.1
  82.0 2.2 constant_dynamic-update-slice_fusion
  84.1 0.0 slice-done
  84.1 0.0 slice-done.1
  84.1 13.5 %fusion.3 = f32[512,2048]{1,0:T(8,128)} fusion(bf16[3584,1024]{1,0:T(8,128)(2,1)S(1)} %bitcast.1, bf16[3584,1024]{1,0:T(8,128)(2,1)} %param.7, bf16[3584,1024]{1,0:T(8,128)(2,1)} %constant_dynamic-update-slice_fusion, s32[]{:T(128)S(6)} %select_n.14), kind=kOutput, calls=%fused_computation.5 | convolution fusion | flops 7545552896 | bytes 22544388 | tf_op jit(solution)/shard_map/dot_general | solution.py:38
  97.7 0.0 all-reduce.2.cloned.1.call-update
  97.7 0.0 all-gather.2.cloned.1.call-done
  97.7 81.0 %all-reduce.2.cloned.1.call-done = f32[512,2048]{1,0:T(8,128)} async-done(((f32[512,2048]{1,0:T(8,128)}), f32[512,2048]{1,0:T(8,128)}) %all-reduce.2.cloned.1.call-update) | async-done | bytes 4194320 | tf_op jit(solution)/shard_map/psum | solution.py:41
  178.7 0.0 slice-start.2
  178.7 0.0 slice-start.4
  178.7 4.3 %fusion.14 = (bf16[512,1024]{1,0:T(8,128)(2,1)S(1)}, bf16[512,1024]{1,0:T(8,128)(2,1)}) fusion(f32[512,2048]{1,0:T(8,128)} %all-reduce.2.cloned.1.call-done, bf16[512,1024]{1,0:T(8,128)(2,1)} %all-gather.2.cloned.1.call-done), kind=kLoop, calls=%fused_computation.19 | loop fusion | flops 3145728 | bytes 7340032 | tf_op jit(solution)/shard_map/convert_element_type | solution.py:26
  183.0 0.0 slice-start.3
  183.0 0.0 slice-start.5
  183.0 15.5 %fusion.8 = f32[3584,2048]{1,0:T(8,128)} fusion(bf16[3584,1024]{1,0:T(8,128)(2,1)} %constant_dynamic-update-slice_fusion, s32[]{:T(128)S(6)} %select_n.14, bf16[512,1024]{1,0:T(8,128)(2,1)} %get-tuple-element.7, bf16[512,1024]{1,0:T(8,128)(2,1)S(1)} %get-tuple-element.6), kind=kOutput, calls=%fused_computation.11 | convolution fusion | flops 7520387072 | bytes 35127300 | tf_op jit(solution)/shard_map/dot_general | solution.py:44
  198.4 0.0 slice-done.2
  198.4 0.0 slice-done.4
  198.4 0.0 slice-done.3
  198.4 0.0 slice-done.5
  198.5 20.9 %clamp_convert_fusion = (bf16[3584,1024]{1,0:T(8,128)(2,1)}, bf16[3584,1024]{1,0:T(8,128)(2,1)}, bf16[3584,1024]{1,0:T(8,128)(2,1)}) fusion(f32[3584,2048]{1,0:T(8,128)} %fusion.8, bf16[3584,1024]{1,0:T(8,128)(2,1)S(1)} %bitcast.5, bf16[3584,1024]{1,0:T(8,128)(2,1)S(1)} %bitcast.3, bf16[3584,1024]{1,0:T(8,128)(2,1)} %param.10), kind=kLoop, calls=%fused_computation.9 | loop fusion | flops 62390272 | bytes 73400320 | tf_op jit(solution)/shard_map/convert_element_type | solution.py:55
  (3 shorter events, 0.0 us)
Async XLA Ops:
  7.2 90.6 %all-gather.2.cloned.1.call-start = ((), (), s32[]{:S(2)}) async-start(), calls=%async_computation.1 | async-start | bytes 1179648 | tf_op jit(solution)/shard_map/all_gather | solution.py:42
  7.2 25.8 %collective-permute-start = (bf16[3584,128]{1,0:T(8,128)(2,1)}, bf16[3584,128]{1,0:T(8,128)(2,1)}, u32[]{:S(2)}, u32[]{:S(2)}) collective-permute-start(bf16[3584,128]{1,0:T(8,128)(2,1)} %param.6), channel_id=1, source_target_pairs={{0,1},{1,2},{2,3},{3,0},{4,5},{5,6},{6,7},{7,4},{8,9},{9,10},{10,1... | collective-permute-start | bytes 2752520 | tf_op jit(solution)/shard_map/ppermute | solution.py:18
  33.0 25.4 %collective-permute-start.1 = (bf16[3584,128]{1,0:T(8,128)(2,1)}, bf16[3584,128]{1,0:T(8,128)(2,1)}, u32[]{:S(2)}, u32[]{:S(2)}) collective-permute-start(bf16[3584,128]{1,0:T(8,128)(2,1)} %collective-permute-done), channel_id=1, source_target_pairs={{0,1},{1,2},{2,3},{3,0},{4,5},{5,6},{6,7},{7,4},{8,9},{9,10},{10,1... | collective-permute-start | bytes 2752520 | tf_op jit(solution)/shard_map/ppermute | solution.py:18
  33.0 41.5 %collective-permute-start.2 = (bf16[3584,128]{1,0:T(8,128)(2,1)}, bf16[3584,128]{1,0:T(8,128)(2,1)}, u32[]{:S(2)}, u32[]{:S(2)}) collective-permute-start(bf16[3584,128]{1,0:T(8,128)(2,1)} %param.6), channel_id=1, source_target_pairs={{0,3},{1,0},{2,1},{3,2},{4,7},{5,4},{6,5},{7,6},{8,11},{9,8},{10,9... | collective-permute-start | bytes 2752520 | tf_op jit(solution)/shard_map/ppermute | solution.py:20
  36.8 141.9 %all-reduce.2.cloned.1.call-start = ((), (), s32[]{:S(2)}) async-start(), calls=%async_computation | async-start | bytes 8388608 | tf_op jit(solution)/shard_map/psum | solution.py:41
  36.9 47.2 %slice-start = ((s8[7340032]{0:T(1024)(128)(4,1)}), s8[3145728]{0:T(1024)(128)(4,1)S(1)}, s32[]{:S(2)}) async-start(s8[7340032]{0:T(1024)(128)(4,1)} %bitcast), calls=%async_computation.2 | async-start | bytes 6291456
  36.9 44.1 %copy-start = (bf16[3584,128]{1,0:T(8,128)(2,1)S(1)}, bf16[3584,128]{1,0:T(8,128)(2,1)}, u32[]{:S(2)}) copy-start(bf16[3584,128]{1,0:T(8,128)(2,1)} %param.6) | copy-start | bytes 2752516
  64.9 19.3 %slice-start.1 = ((s8[7340032]{0:T(1024)(128)(4,1)}), s8[4194304]{0:T(1024)(128)(4,1)S(1)}, s32[]{:S(2)}) async-start(s8[7340032]{0:T(1024)(128)(4,1)} %bitcast), calls=%async_computation.3 | async-start | bytes 8388608
  178.7 19.8 %slice-start.2 = ((s8[7340032]{0:T(1024)(128)(4,1)}), s8[4194304]{0:T(1024)(128)(4,1)S(1)}, s32[]{:S(2)}) async-start(s8[7340032]{0:T(1024)(128)(4,1)} %bitcast.2), calls=%async_computation.4 | async-start | bytes 8388608
  178.7 19.8 %slice-start.4 = ((s8[7340032]{0:T(1024)(128)(4,1)}), s8[4194304]{0:T(1024)(128)(4,1)S(1)}, s32[]{:S(2)}) async-start(s8[7340032]{0:T(1024)(128)(4,1)} %bitcast.4), calls=%async_computation.6 | async-start | bytes 8388608
  183.0 15.5 %slice-start.3 = ((s8[7340032]{0:T(1024)(128)(4,1)}), s8[3145728]{0:T(1024)(128)(4,1)S(1)}, s32[]{:S(2)}) async-start(s8[7340032]{0:T(1024)(128)(4,1)} %bitcast.2), calls=%async_computation.5 | async-start | bytes 6291456
  183.0 15.5 %slice-start.5 = ((s8[7340032]{0:T(1024)(128)(4,1)}), s8[3145728]{0:T(1024)(128)(4,1)S(1)}, s32[]{:S(2)}) async-start(s8[7340032]{0:T(1024)(128)(4,1)} %bitcast.4), calls=%async_computation.7 | async-start | bytes 6291456
Sparse Core Ops, SparseCore 0:
  36.9 21.6 all-gather.1
  97.8 80.8 all-reduce.1
